TPU v7x, 256 devices: a whole 4x4x8 slice. The times are simulated.
256 devices in a mesh: section: 8 (over y, core), seq: 32 (over x, z).
Axes of the slice: x: 4, y: 4, z: 8, core: 2. Of those that a mesh axis runs over, the one named last changes fastest.
Arguments:
- queries: bfloat16 [8, 8192, 2560], P('section', 'seq'), may hold values from -200 to 200
- keys: bfloat16 [8, 8192, 512], P('section', 'seq'), may hold values from -4 to 4
- values: bfloat16 [8, 8192, 512], P('section', 'seq'), may hold values from -6 to 6
- lengths: int32 [8, 64], P('section'), may hold values from 1 to 1024, 8192 in all within a row
Outputs:
- handed: bfloat16 [8, 8192, 2560], P('section', 'seq')
Inputs may be any that keep to these rules, and one draw needn't show every extreme that they name: `lengths`: each row sums to 8192; its longest episode has exactly 1024 positions.
All inputs are finite; a program needn't handle non-finite values.
Results may differ from a plain program's by a relative error of at most 0.003.
Values may be sent and summed in bfloat16 or wider, within the bound.
No kernel may reach another device: no remote copies, remote signals or barrier semaphores. Data moves between devices by JAX's collectives and lax.ppermute only.
A program may use at most 128 MiB of HBM per device.

v0:
```python
from functools import partial

import jax
import jax.numpy as jnp
from jax import lax
from jax.experimental import pallas as pl
from jax.experimental.pallas import tpu as pltpu
from jax.sharding import PartitionSpec as P

HDIM = 128
KV_HEADS = 4
GROUP = 5
RING = 8
LOWEST = -1e30
SCALE = HDIM**-0.5 * 1.4426950408889634


def moved(value, route):
    sections, blocks = lax.axis_size("section"), lax.axis_size("seq")
    pairs = []
    for s in range(sections):
        for b in range(blocks):
            s2, b2 = route(s, b)
            pairs.append((s * blocks + b, (s2 % sections) * blocks + b2 % blocks))
    return lax.ppermute(value, ("section", "seq"), pairs)


def step(blocks, sections=0):
    return lambda s, b: (s + sections, b + blocks)


def back_two(s, b):
    x, z = divmod(b + 4, RING)
    return s + 1, x * RING + (z + 2) % RING


def back_four(s, b):
    x, u = divmod(b, RING)
    return s, x * RING + (u - 2) % RING


def bias_of(starts, first_key, height):
    keys = first_key + lax.broadcasted_iota(jnp.int32, (height, height), 1)
    return jnp.where(keys >= starts, 0.0, LOWEST)


def tile(q, k, v, bias):
    height = bias.shape[0]
    raw = lax.dot_general(q, k, (((1,), (1,)), ((), ())), preferred_element_type=jnp.float32)
    raw = (raw.reshape(GROUP, height, height) + bias[None]).reshape(GROUP * height, height)
    top = jnp.max(raw, axis=1, keepdims=True)
    weights = jnp.exp2((raw - top) * SCALE)
    total = jnp.sum(weights, axis=1, keepdims=True)
    out = jnp.dot(weights.astype(jnp.bfloat16), v, preferred_element_type=jnp.float32)
    wide = (GROUP * height, HDIM)
    return out, jnp.broadcast_to(top, wide), jnp.broadcast_to(total, wide)


def merged(terms):
    highest = terms[0][1]
    for item in terms[1:]:
        highest = jnp.maximum(highest, item[1])
    out, total = None, None
    for tile_out, top, tile_sum in terms:
        factor = jnp.exp2((top - highest) * SCALE)
        part, part_sum = tile_out * factor, tile_sum * factor
        out = part if out is None else out + part
        total = part_sum if total is None else total + part_sum
    return out, highest, total


def kernel(backs, opening, closing, starts_ref, q_ref, *refs):
    count = len(backs)
    ks, vs, refs = refs[:count], refs[count : 2 * count], refs[2 * count :]
    state_in = () if opening else refs[:3]
    outs, bias_ref = refs[len(state_in) : -1], refs[-1]
    height = q_ref.shape[0]
    lane = lax.broadcasted_iota(jnp.int32, (height, HDIM), 1)
    digits = starts_ref[...].astype(jnp.float32) * jnp.where(lane == 0, 32.0, 1.0)
    distance = jnp.sum(digits, axis=1, keepdims=True).astype(jnp.int32)
    starts = lax.broadcasted_iota(jnp.int32, (height, 1), 0) - distance
    reach = jnp.sum(digits[:1]).astype(jnp.int32)

    def run(taken):
        for i in taken:
            back = backs[i]
            bias = bias_of(starts, -back * height, height)
            if back == 0:
                rows = lax.broadcasted_iota(jnp.int32, (height, height), 0)
                columns = lax.broadcasted_iota(jnp.int32, (height, height), 1)
                bias = jnp.where(columns <= rows, bias, LOWEST)
            bias_ref[i] = bias

        @pl.loop(0, KV_HEADS, unroll=KV_HEADS)
        def _(a):
            lanes = pl.ds(pl.multiple_of(a * HDIM, HDIM), HDIM)
            heads = [pl.ds(pl.multiple_of((a * GROUP + g) * HDIM, HDIM), HDIM) for g in range(GROUP)]
            terms = [tuple(ref[a] for ref in state_in)] if state_in else []
            if taken:
                q = jnp.concatenate([q_ref[:, h] for h in heads], axis=0)
                terms += [tile(q, ks[i][:, lanes], vs[i][:, lanes], bias_ref[i]) for i in taken]
            result = merged(terms)
            if closing:
                done = (result[0] / result[2]).astype(jnp.bfloat16)
                for g in range(GROUP):
                    outs[0][:, heads[g]] = done[g * height : (g + 1) * height]
            else:
                for ref, part in zip(outs, result):
                    ref[a] = part

    least = 1 if opening else 0
    for taken in range(least, count + 1):
        low = reach > (backs[taken - 1] - 1) * height if taken > least else True
        high = reach <= (backs[taken] - 1) * height if taken < count else True
        pl.when(jnp.logical_and(low, high))(partial(run, tuple(range(taken))))


def attention(backs, starts, q, ks, vs, state=(), closing=False):
    height = q.shape[0]
    count = len(backs)
    pairs = KV_HEADS * GROUP * height * height * count
    vmem = pl.BlockSpec(memory_space=pltpu.VMEM)
    part = jax.ShapeDtypeStruct((KV_HEADS, GROUP * height, HDIM), jnp.float32)
    first = 2 + 2 * count
    return pl.pallas_call(
        partial(kernel, backs, not state, closing),
        in_specs=[vmem] * (first + len(state)),
        out_specs=vmem if closing else [vmem] * 3,
        out_shape=jax.ShapeDtypeStruct(q.shape, jnp.bfloat16) if closing else [part] * 3,
        input_output_aliases={first + i: i for i in range(len(state))} if not closing else {},
        scratch_shapes=[pltpu.VMEM((count, height, height), jnp.float32)],
        compiler_params=pltpu.CompilerParams(vmem_limit_bytes=14 << 20),
        cost_estimate=pl.CostEstimate(
            flops=4 * HDIM * pairs, transcendentals=pairs, bytes_accessed=8 << 20
        ),
        name="tiles_" + "_".join(str(back) for back in backs),
    )(starts, q, *ks, *vs, *state)


def distances(sizes, positions):
    order = jnp.arange(sizes.shape[0], dtype=jnp.int32)
    begins = jnp.sum(jnp.where(order[:, None] < order[None, :], sizes[:, None], 0), axis=0, dtype=jnp.int32)
    inside = begins[None, :] <= positions[:, None]
    distance = positions - jnp.max(jnp.where(inside, begins[None, :], 0), axis=1)
    lane = jnp.arange(HDIM, dtype=jnp.int32)[None, :]
    digits = jnp.where(lane == 0, distance[:, None] // 32, jnp.where(lane == 1, distance[:, None] % 32, 0))
    return digits.astype(jnp.bfloat16)


def body(queries, keys, values, lengths):
    q, k, v = queries[0], keys[0], values[0]
    height = q.shape[0]
    index = lax.axis_index("seq").astype(jnp.int32)

    width = k.shape[1]
    positions = index * height + jnp.arange(height, dtype=jnp.int32)
    v_far = moved(v, back_two)
    k1 = moved(k, step(1, 1))
    v1 = moved(v, step(1, 1))
    sizes = lengths[0]
    q0 = moved(q, step(0, 1))
    k, v, sizes, k1 = lax.optimization_barrier((k, v, sizes, k1))
    k0 = moved(k, step(0, 1))
    near = moved(jnp.concatenate([v, distances(sizes, positions)], axis=1), step(0, 1))
    v0, starts = near[:, :width], near[:, width:]
    k2 = moved(k1, step(1))
    v4 = moved(v_far, back_four)
    v2 = moved(v1, step(1))
    k2, v_far, v1 = lax.optimization_barrier((k2, v_far, v1))
    k3 = moved(k2, step(1))
    v3 = moved(v4, step(-1))
    k3, v2 = lax.optimization_barrier((k3, v2))
    k3, k0 = lax.optimization_barrier((k3, k0))
    k4 = moved(k3, step(1))
    state = attention((0, 1, 2), starts, q0, [k0, k1, k2], [v0, v1, v2])
    return attention((3, 4), starts, q0, [k3, k4], [v3, v4], state, True)[None]


def solution(mesh):
    return jax.shard_map(
        body,
        mesh=mesh,
        in_specs=(
            P("section", "seq", None),
            P("section", "seq", None),
            P("section", "seq", None),
            P("section", None),
        ),
        out_specs=P("section", "seq", None),
        check_vma=False,
    )
```

profile of v0, /device:TPU:4, one launch (start us, length us, event | category | flops | bytes accessed | tf_op | source)
XLA Modules:
  0.0 53.2 jit_solution(13959914567364173885)
XLA Ops:
  0.0 1.4 %collective-permute-start = (bf16[256,512]{1,0:T(8,128)(2,1)}, bf16[256,512]{1,0:T(8,128)(2,1)S(1)}, u32[]{:S(2)}, u32[]{:S(2)}) collective-permute-start(bf16[256,512]{1,0:T(8,128)(2,1)} %bitcast.9), channel_id=1, source_target_pairs={{0,33},{1,34},{2,35},{3,36},{4,37},{5,38},{6,39},{7,40},{8,41},{9,... | collective-permute-start | bytes 786440 | tf_op jit(solution)/shard_map/ppermute | solution.py:25
  1.4 6.7 %collective-permute-start.4 = (bf16[256,512]{1,0:T(8,128)(2,1)}, bf16[256,512]{1,0:T(8,128)(2,1)S(1)}, u32[]{:S(2)}, u32[]{:S(2)}) collective-permute-start(bf16[256,512]{1,0:T(8,128)(2,1)} %bitcast.5), channel_id=1, source_target_pairs={{0,38},{1,39},{2,32},{3,33},{4,42},{5,43},{6,44},{7,45},{8,46},{9,... | collective-permute-start | bytes 786440 | tf_op jit(solution)/shard_map/ppermute | solution.py:25
  8.1 0.0 collective-permute-start.5
  8.1 0.0 collective-permute-start.2
  8.1 6.0 %collective-permute-done.refs_1_ = bf16[256,512]{1,0:T(8,128)(2,1)S(1)} collective-permute-done((bf16[256,512]{1,0:T(8,128)(2,1)}, bf16[256,512]{1,0:T(8,128)(2,1)S(1)}, u32[]{:S(2)}, u32[]{:S(2)}) %collective-permute-start) | collective-permute-done | bytes 262176 | tf_op jit(solution)/shard_map/ppermute | solution.py:25
  14.1 0.0 collective-permute-start.3
  14.1 0.7 %select_reduce_fusion.1 = s32[64]{0:T(128)S(1)} fusion(s32[64]{0:T(128)} %bitcast.11), kind=kLoop, calls=%fused_computation.3 | loop fusion | flops 12224 | bytes 512 | tf_op jit(solution)/shard_map/reduce_sum | solution.py:142
  14.8 0.1 select_reduce_fusion
  14.9 0.0 collective-permute-start.8
  15.0 5.9 %collective-permute-done.5.refs_4_ = bf16[256,512]{1,0:T(8,128)(2,1)S(1)} collective-permute-done((bf16[256,512]{1,0:T(8,128)(2,1)}, bf16[256,512]{1,0:T(8,128)(2,1)S(1)}, u32[]{:S(2)}, u32[]{:S(2)}) %collective-permute-start.5) | collective-permute-done | bytes 262176 | tf_op jit(solution)/shard_map/ppermute | solution.py:25
  20.9 0.0 collective-permute-start.7
  20.9 0.0 collective-permute-done.4
  20.9 4.0 %collective-permute-start.10 = (bf16[256,512]{1,0:T(8,128)(2,1)S(1)}, bf16[256,512]{1,0:T(8,128)(2,1)S(1)}, u32[]{:S(2)}, u32[]{:S(2)}) collective-permute-start(bf16[256,512]{1,0:T(8,128)(2,1)S(1)} %collective-permute-done.4), channel_id=1, source_target_pairs={{0,6},{1,7},{2,0},{3,1},{4,2},{5,3},{6,4},{7,5},{8,14},{9,15},{10,... | collective-permute-start | bytes 786440 | tf_op jit(solution)/shard_map/ppermute | solution.py:25
  24.8 0.1 select_convert_fusion
  25.0 0.4 collective-permute-done.3.refs_2_
  25.4 1.3 %collective-permute-start.6 = (bf16[256,512]{1,0:T(8,128)(2,1)S(1)}, bf16[256,512]{1,0:T(8,128)(2,1)S(1)}, u32[]{:S(2)}, u32[]{:S(2)}) collective-permute-start(bf16[256,512]{1,0:T(8,128)(2,1)S(1)} %collective-permute-done.3.refs_2_), channel_id=1, source_target_pairs={{0,1},{1,2},{2,3},{3,4},{4,5},{5,6},{6,7},{7,8},{8,9},{9,10},{10,1... | collective-permute-start | bytes 786440 | tf_op jit(solution)/shard_map/ppermute | solution.py:25
  26.7 1.0 %pad_maximum_fusion = bf16[256,640]{1,0:T(8,128)(2,1)S(1)} fusion(bf16[256,128]{1,0:T(8,128)(2,1)S(1)} %select_convert_fusion, bf16[256,512]{1,0:T(8,128)(2,1)} %bitcast.7), kind=kLoop, calls=%fused_computation | loop fusion | flops 655360 | bytes 655360 | tf_op jit(solution)/shard_map/concatenate | solution.py:164
  27.7 4.0 %collective-permute-done.7.refs_5_ = bf16[256,512]{1,0:T(8,128)(2,1)S(1)} collective-permute-done((bf16[256,512]{1,0:T(8,128)(2,1)S(1)}, bf16[256,512]{1,0:T(8,128)(2,1)S(1)}, u32[]{:S(2)}, u32[]{:S(2)}) %collective-permute-start.7) | collective-permute-done | bytes 262176 | tf_op jit(solution)/shard_map/ppermute | solution.py:25
  31.7 0.0 collective-permute-start.1
  31.7 3.6 %collective-permute-done.10.refs_3_ = bf16[256,512]{1,0:T(8,128)(2,1)S(1)} collective-permute-done((bf16[256,512]{1,0:T(8,128)(2,1)S(1)}, bf16[256,512]{1,0:T(8,128)(2,1)S(1)}, u32[]{:S(2)}, u32[]{:S(2)}) %collective-permute-start.10) | collective-permute-done | bytes 262176 | tf_op jit(solution)/shard_map/ppermute | solution.py:25
  35.3 2.2 %collective-permute-start.11 = (bf16[256,512]{1,0:T(8,128)(2,1)S(1)}, bf16[256,512]{1,0:T(8,128)(2,1)S(1)}, u32[]{:S(2)}, u32[]{:S(2)}) collective-permute-start(bf16[256,512]{1,0:T(8,128)(2,1)S(1)} %collective-permute-done.10.refs_3_), channel_id=1, source_target_pairs={{0,31},{1,0},{2,1},{3,2},{4,3},{5,4},{6,5},{7,6},{8,7},{9,8},{10,9... | collective-permute-start | bytes 786440 | tf_op jit(solution)/shard_map/ppermute | solution.py:25
  37.5 0.0 collective-permute-done.6.refs_0_
  37.5 0.0 collective-permute-done.8.refs_0_
  37.5 0.3 collective-permute-start.9
  37.8 1.7 %collective-permute-done.1 = bf16[256,640]{1,0:T(8,128)(2,1)S(1)} collective-permute-done((bf16[256,640]{1,0:T(8,128)(2,1)S(1)}, bf16[256,640]{1,0:T(8,128)(2,1)S(1)}, u32[]{:S(2)}, u32[]{:S(2)}) %collective-permute-start.1) | collective-permute-done | bytes 327712 | tf_op jit(solution)/shard_map/ppermute | solution.py:25
  39.5 0.0 collective-permute-done.2.q_ref
  39.5 7.0 %tiles_0_1_2.1 = (f32[4,1280,128]{2,1,0:T(8,128)S(1)}, f32[4,1280,128]{2,1,0:T(8,128)S(1)}, f32[4,1280,128]{2,1,0:T(8,128)S(1)}) custom-call(bf16[256,128]{1,0:T(8,128)(2,1)S(1)} %slice.8.starts_ref, bf16[256,2560]{1,0:T(8,128)(2,1)S(1)} %collective-permute-done.2.q_ref, bf16[256,512]{1,0:T(8,128)(2,1)S(1)} %collective-permute-done.8.refs_0_, ...), custom_call_target="tpu_custom_call" | custom-call | flops 2013265920 | bytes 8388608 | tf_op jit(solution)/shard_map/tiles_0_1_2/pallas_call | solution.py:125
  46.5 0.0 collective-permute-done.11.refs_2_
  46.5 0.0 collective-permute-done.9.refs_1_
  46.5 6.8 %tiles_3_4.1 = bf16[256,2560]{1,0:T(8,128)(2,1)} custom-call(bf16[256,128]{1,0:T(8,128)(2,1)S(1)} %slice.8.starts_ref, bf16[256,2560]{1,0:T(8,128)(2,1)S(1)} %collective-permute-done.2.q_ref, bf16[256,512]{1,0:T(8,128)(2,1)S(1)} %collective-permute-done.6.refs_0_, bf16[256,512]{1,0:T(8,128)(2,1)S(1)} %collective-permute-done.9.refs_1_, ...), custom_call_target="tpu_custom_call" | custom-call | flops 1342177280 | bytes 8388608 | tf_op jit(solution)/shard_map/tiles_3_4/pallas_call | solution.py:125
  (5 shorter events, 0.1 us)
Async XLA Ops:
  0.0 14.1 %collective-permute-start = (bf16[256,512]{1,0:T(8,128)(2,1)}, bf16[256,512]{1,0:T(8,128)(2,1)S(1)}, u32[]{:S(2)}, u32[]{:S(2)}) collective-permute-start(bf16[256,512]{1,0:T(8,128)(2,1)} %bitcast.9), channel_id=1, source_target_pairs={{0,33},{1,34},{2,35},{3,36},{4,37},{5,38},{6,39},{7,40},{8,41},{9,... | collective-permute-start | bytes 786440 | tf_op jit(solution)/shard_map/ppermute | solution.py:25
  1.4 19.5 %collective-permute-start.4 = (bf16[256,512]{1,0:T(8,128)(2,1)}, bf16[256,512]{1,0:T(8,128)(2,1)S(1)}, u32[]{:S(2)}, u32[]{:S(2)}) collective-permute-start(bf16[256,512]{1,0:T(8,128)(2,1)} %bitcast.5), channel_id=1, source_target_pairs={{0,38},{1,39},{2,32},{3,33},{4,42},{5,43},{6,44},{7,45},{8,46},{9,... | collective-permute-start | bytes 786440 | tf_op jit(solution)/shard_map/ppermute | solution.py:25
  8.1 12.8 %collective-permute-start.5 = (bf16[256,512]{1,0:T(8,128)(2,1)}, bf16[256,512]{1,0:T(8,128)(2,1)S(1)}, u32[]{:S(2)}, u32[]{:S(2)}) collective-permute-start(bf16[256,512]{1,0:T(8,128)(2,1)} %bitcast.6), channel_id=1, source_target_pairs={{0,33},{1,34},{2,35},{3,36},{4,37},{5,38},{6,39},{7,40},{8,41},{9,... | collective-permute-start | bytes 786440 | tf_op jit(solution)/shard_map/ppermute | solution.py:25
  8.1 31.4 %collective-permute-start.2 = (bf16[256,2560]{1,0:T(8,128)(2,1)}, bf16[256,2560]{1,0:T(8,128)(2,1)S(1)}, u32[]{:S(2)}, u32[]{:S(2)}) collective-permute-start(bf16[256,2560]{1,0:T(8,128)(2,1)} %bitcast.8), channel_id=1, source_target_pairs={{0,32},{1,33},{2,34},{3,35},{4,36},{5,37},{6,38},{7,39},{8,40},{9,... | collective-permute-start | bytes 3932168 | tf_op jit(solution)/shard_map/ppermute | solution.py:25
  14.1 11.4 %collective-permute-start.3 = (bf16[256,512]{1,0:T(8,128)(2,1)S(1)}, bf16[256,512]{1,0:T(8,128)(2,1)S(1)}, u32[]{:S(2)}, u32[]{:S(2)}) collective-permute-start(bf16[256,512]{1,0:T(8,128)(2,1)S(1)} %collective-permute-done.refs_1_), channel_id=1, source_target_pairs={{0,1},{1,2},{2,3},{3,4},{4,5},{5,6},{6,7},{7,8},{8,9},{9,10},{10,1... | collective-permute-start | bytes 786440 | tf_op jit(solution)/shard_map/ppermute | solution.py:25
  14.9 22.5 %collective-permute-start.8 = (bf16[256,512]{1,0:T(8,128)(2,1)}, bf16[256,512]{1,0:T(8,128)(2,1)S(1)}, u32[]{:S(2)}, u32[]{:S(2)}) collective-permute-start(bf16[256,512]{1,0:T(8,128)(2,1)} %bitcast.10), channel_id=1, source_target_pairs={{0,32},{1,33},{2,34},{3,35},{4,36},{5,37},{6,38},{7,39},{8,40},{9,... | collective-permute-start | bytes 786440 | tf_op jit(solution)/shard_map/ppermute | solution.py:25
  20.9 10.9 %collective-permute-start.7 = (bf16[256,512]{1,0:T(8,128)(2,1)S(1)}, bf16[256,512]{1,0:T(8,128)(2,1)S(1)}, u32[]{:S(2)}, u32[]{:S(2)}) collective-permute-start(bf16[256,512]{1,0:T(8,128)(2,1)S(1)} %collective-permute-done.5.refs_4_), channel_id=1, source_target_pairs={{0,1},{1,2},{2,3},{3,4},{4,5},{5,6},{6,7},{7,8},{8,9},{9,10},{10,1... | collective-permute-start | bytes 786440 | tf_op jit(solution)/shard_map/ppermute | solution.py:25
  20.9 14.4 %collective-permute-start.10 = (bf16[256,512]{1,0:T(8,128)(2,1)S(1)}, bf16[256,512]{1,0:T(8,128)(2,1)S(1)}, u32[]{:S(2)}, u32[]{:S(2)}) collective-permute-start(bf16[256,512]{1,0:T(8,128)(2,1)S(1)} %collective-permute-done.4), channel_id=1, source_target_pairs={{0,6},{1,7},{2,0},{3,1},{4,2},{5,3},{6,4},{7,5},{8,14},{9,15},{10,... | collective-permute-start | bytes 786440 | tf_op jit(solution)/shard_map/ppermute | solution.py:25
  25.4 12.0 %collective-permute-start.6 = (bf16[256,512]{1,0:T(8,128)(2,1)S(1)}, bf16[256,512]{1,0:T(8,128)(2,1)S(1)}, u32[]{:S(2)}, u32[]{:S(2)}) collective-permute-start(bf16[256,512]{1,0:T(8,128)(2,1)S(1)} %collective-permute-done.3.refs_2_), channel_id=1, source_target_pairs={{0,1},{1,2},{2,3},{3,4},{4,5},{5,6},{6,7},{7,8},{8,9},{9,10},{10,1... | collective-permute-start | bytes 786440 | tf_op jit(solution)/shard_map/ppermute | solution.py:25
  31.7 7.7 %collective-permute-start.1 = (bf16[256,640]{1,0:T(8,128)(2,1)S(1)}, bf16[256,640]{1,0:T(8,128)(2,1)S(1)}, u32[]{:S(2)}, u32[]{:S(2)}) collective-permute-start(bf16[256,640]{1,0:T(8,128)(2,1)S(1)} %pad_maximum_fusion), channel_id=1, source_target_pairs={{0,32},{1,33},{2,34},{3,35},{4,36},{5,37},{6,38},{7,39},{8,40},{9,... | collective-permute-start | bytes 983048 | tf_op jit(solution)/shard_map/ppermute | solution.py:25
  35.3 11.2 %collective-permute-start.11 = (bf16[256,512]{1,0:T(8,128)(2,1)S(1)}, bf16[256,512]{1,0:T(8,128)(2,1)S(1)}, u32[]{:S(2)}, u32[]{:S(2)}) collective-permute-start(bf16[256,512]{1,0:T(8,128)(2,1)S(1)} %collective-permute-done.10.refs_3_), channel_id=1, source_target_pairs={{0,31},{1,0},{2,1},{3,2},{4,3},{5,4},{6,5},{7,6},{8,7},{9,8},{10,9... | collective-permute-start | bytes 786440 | tf_op jit(solution)/shard_map/ppermute | solution.py:25
  37.5 9.0 %collective-permute-start.9 = (bf16[256,512]{1,0:T(8,128)(2,1)S(1)}, bf16[256,512]{1,0:T(8,128)(2,1)S(1)}, u32[]{:S(2)}, u32[]{:S(2)}) collective-permute-start(bf16[256,512]{1,0:T(8,128)(2,1)S(1)} %collective-permute-done.6.refs_0_), channel_id=1, source_target_pairs={{0,1},{1,2},{2,3},{3,4},{4,5},{5,6},{6,7},{7,8},{8,9},{9,10},{10,1... | collective-permute-start | bytes 786440 | tf_op jit(solution)/shard_map/ppermute | solution.py:25
where the time goes:
time: 53.8 us; the launch traced here: 53.2 us
  waiting for transfers between devices  21.6 us (40%)
  starting transfers between devices  15.8 us (29%)
  Pallas kernels  13.7 us (25%)
  other arithmetic  1.98 us (4%)
    ppermute x12, waiting for transfers between devices, moved(): return lax.ppermute(value, ('section', 'seq'), pairs)  21.6 us
    ppermute x12, starting transfers between devices, moved(): return lax.ppermute(value, ('section', 'seq'), pairs)  15.8 us
    pallas_call x2, Pallas kernels, attention(): pl.pallas_call(partial(kernel, backs, not state, closing), in_specs=[vmem...  13.7 us
  transfers between devices with their start and end apart: 12, of which 6 were waited for; matrix products, arithmetic and copies ran while one was open for 4% of the time, Pallas kernels for 13%

commit v1 on v0

--- a/solution.py
+++ b/solution.py
@@ -45,14 +45,14 @@
 
 
 def tile(q, k, v, bias):
-    height = bias.shape[0]
+    rows, keys = bias.shape
     raw = lax.dot_general(q, k, (((1,), (1,)), ((), ())), preferred_element_type=jnp.float32)
-    raw = (raw.reshape(GROUP, height, height) + bias[None]).reshape(GROUP * height, height)
+    raw = (raw.reshape(GROUP, rows, keys) + bias[None]).reshape(GROUP * rows, keys)
     top = jnp.max(raw, axis=1, keepdims=True)
     weights = jnp.exp2((raw - top) * SCALE)
     total = jnp.sum(weights, axis=1, keepdims=True)
     out = jnp.dot(weights.astype(jnp.bfloat16), v, preferred_element_type=jnp.float32)
-    wide = (GROUP * height, HDIM)
+    wide = (GROUP * rows, HDIM)
     return out, jnp.broadcast_to(top, wide), jnp.broadcast_to(total, wide)
 
 
@@ -79,40 +79,47 @@
     digits = starts_ref[...].astype(jnp.float32) * jnp.where(lane == 0, 32.0, 1.0)
     distance = jnp.sum(digits, axis=1, keepdims=True).astype(jnp.int32)
     starts = lax.broadcasted_iota(jnp.int32, (height, 1), 0) - distance
-    reach = jnp.sum(digits[:1]).astype(jnp.int32)
 
-    def run(taken):
+    def run(taken, row, rows):
         for i in taken:
             back = backs[i]
             bias = bias_of(starts, -back * height, height)
             if back == 0:
-                rows = lax.broadcasted_iota(jnp.int32, (height, height), 0)
+                own = lax.broadcasted_iota(jnp.int32, (height, height), 0)
                 columns = lax.broadcasted_iota(jnp.int32, (height, height), 1)
-                bias = jnp.where(columns <= rows, bias, LOWEST)
+                bias = jnp.where(columns <= own, bias, LOWEST)
             bias_ref[i] = bias
 
         @pl.loop(0, KV_HEADS, unroll=KV_HEADS)
         def _(a):
             lanes = pl.ds(pl.multiple_of(a * HDIM, HDIM), HDIM)
             heads = [pl.ds(pl.multiple_of((a * GROUP + g) * HDIM, HDIM), HDIM) for g in range(GROUP)]
-            terms = [tuple(ref[a] for ref in state_in)] if state_in else []
+            part = [pl.ds(g * height + row, rows) for g in range(GROUP)]
+            terms = []
+            if state_in:
+                terms.append([jnp.concatenate([ref[a, p] for p in part], axis=0) for ref in state_in])
             if taken:
-                q = jnp.concatenate([q_ref[:, h] for h in heads], axis=0)
-                terms += [tile(q, ks[i][:, lanes], vs[i][:, lanes], bias_ref[i]) for i in taken]
+                q = jnp.concatenate([q_ref[row : row + rows, h] for h in heads], axis=0)
+                for i in taken:
+                    terms.append(tile(q, ks[i][:, lanes], vs[i][:, lanes], bias_ref[i, row : row + rows]))
             result = merged(terms)
             if closing:
                 done = (result[0] / result[2]).astype(jnp.bfloat16)
                 for g in range(GROUP):
-                    outs[0][:, heads[g]] = done[g * height : (g + 1) * height]
+                    outs[0][row : row + rows, heads[g]] = done[g * rows : (g + 1) * rows]
             else:
-                for ref, part in zip(outs, result):
-                    ref[a] = part
+                for ref, value in zip(outs, result):
+                    for g in range(GROUP):
+                        ref[a, part[g]] = value[g * rows : (g + 1) * rows]
 
     least = 1 if opening else 0
-    for taken in range(least, count + 1):
-        low = reach > (backs[taken - 1] - 1) * height if taken > least else True
-        high = reach <= (backs[taken] - 1) * height if taken < count else True
-        pl.when(jnp.logical_and(low, high))(partial(run, tuple(range(taken))))
+    rows = height // 2 if closing else height
+    for row in range(0, height, rows):
+        reach = jnp.sum(digits[row : row + 1]).astype(jnp.int32) - row
+        for taken in range(least, count + 1):
+            low = reach > (backs[taken - 1] - 1) * height if taken > least else True
+            high = reach <= (backs[taken] - 1) * height if taken < count else True
+            pl.when(jnp.logical_and(low, high))(partial(run, tuple(range(taken)), row, rows))
 
 
 def attention(backs, starts, q, ks, vs, state=(), closing=False):

time: 53.8 us -> 52.4 us (0.974)
  the two profiles are of different devices: /device:TPU:4 before, /device:TPU:8 now
where the time goes in v1:
time: 52.4 us; the launch traced here: 52.3 us
  waiting for transfers between devices  29.4 us (56%)
  starting transfers between devices  16.4 us (31%)
  Pallas kernels  4.4 us (8%)
  other arithmetic  1.98 us (4%)
    ppermute x12, waiting for transfers between devices, moved(): return lax.ppermute(value, ('section', 'seq'), pairs)  29.4 us
    ppermute x12, starting transfers between devices, moved(): return lax.ppermute(value, ('section', 'seq'), pairs)  16.4 us
    pallas_call x2, Pallas kernels, attention(): pl.pallas_call(partial(kernel, backs, not state, closing), in_specs=[vmem...  4.4 us
  transfers between devices with their start and end apart: 12, of which 7 were waited for; matrix products, arithmetic and copies ran while one was open for 4% of the time, Pallas kernels for 4%

profile of v1, /device:TPU:8, one launch (start us, length us, event | category | flops | bytes accessed | tf_op | source)
XLA Modules:
  0.0 52.3 jit_solution(3640353153676090712)
XLA Ops:
  0.0 1.4 %collective-permute-start = (bf16[256,512]{1,0:T(8,128)(2,1)}, bf16[256,512]{1,0:T(8,128)(2,1)S(1)}, u32[]{:S(2)}, u32[]{:S(2)}) collective-permute-start(bf16[256,512]{1,0:T(8,128)(2,1)} %bitcast.9), channel_id=1, source_target_pairs={{0,33},{1,34},{2,35},{3,36},{4,37},{5,38},{6,39},{7,40},{8,41},{9,... | collective-permute-start | bytes 786440 | tf_op jit(solution)/shard_map/ppermute | solution.py:25
  1.4 6.7 %collective-permute-start.4 = (bf16[256,512]{1,0:T(8,128)(2,1)}, bf16[256,512]{1,0:T(8,128)(2,1)S(1)}, u32[]{:S(2)}, u32[]{:S(2)}) collective-permute-start(bf16[256,512]{1,0:T(8,128)(2,1)} %bitcast.5), channel_id=1, source_target_pairs={{0,38},{1,39},{2,32},{3,33},{4,42},{5,43},{6,44},{7,45},{8,46},{9,... | collective-permute-start | bytes 786440 | tf_op jit(solution)/shard_map/ppermute | solution.py:25
  8.1 0.0 collective-permute-start.5
  8.1 0.0 collective-permute-start.2
  8.1 5.6 %collective-permute-done.refs_1_ = bf16[256,512]{1,0:T(8,128)(2,1)S(1)} collective-permute-done((bf16[256,512]{1,0:T(8,128)(2,1)}, bf16[256,512]{1,0:T(8,128)(2,1)S(1)}, u32[]{:S(2)}, u32[]{:S(2)}) %collective-permute-start) | collective-permute-done | bytes 262176 | tf_op jit(solution)/shard_map/ppermute | solution.py:25
  13.7 0.0 collective-permute-start.3
  13.7 0.7 %select_reduce_fusion.1 = s32[64]{0:T(128)S(1)} fusion(s32[64]{0:T(128)} %bitcast.11), kind=kLoop, calls=%fused_computation.3 | loop fusion | flops 12224 | bytes 512 | tf_op jit(solution)/shard_map/reduce_sum | solution.py:149
  14.4 0.1 select_reduce_fusion
  14.6 0.7 %collective-permute-start.8 = (bf16[256,512]{1,0:T(8,128)(2,1)}, bf16[256,512]{1,0:T(8,128)(2,1)S(1)}, u32[]{:S(2)}, u32[]{:S(2)}) collective-permute-start(bf16[256,512]{1,0:T(8,128)(2,1)} %bitcast.10), channel_id=1, source_target_pairs={{0,32},{1,33},{2,34},{3,35},{4,36},{5,37},{6,38},{7,39},{8,40},{9,... | collective-permute-start | bytes 786440 | tf_op jit(solution)/shard_map/ppermute | solution.py:25
  15.3 4.9 %collective-permute-done.5.refs_4_ = bf16[256,512]{1,0:T(8,128)(2,1)S(1)} collective-permute-done((bf16[256,512]{1,0:T(8,128)(2,1)}, bf16[256,512]{1,0:T(8,128)(2,1)S(1)}, u32[]{:S(2)}, u32[]{:S(2)}) %collective-permute-start.5) | collective-permute-done | bytes 262176 | tf_op jit(solution)/shard_map/ppermute | solution.py:25
  20.1 0.0 collective-permute-start.7
  20.1 0.0 collective-permute-done.4
  20.2 3.6 %collective-permute-start.10 = (bf16[256,512]{1,0:T(8,128)(2,1)S(1)}, bf16[256,512]{1,0:T(8,128)(2,1)S(1)}, u32[]{:S(2)}, u32[]{:S(2)}) collective-permute-start(bf16[256,512]{1,0:T(8,128)(2,1)S(1)} %collective-permute-done.4), channel_id=1, source_target_pairs={{0,6},{1,7},{2,0},{3,1},{4,2},{5,3},{6,4},{7,5},{8,14},{9,15},{10,... | collective-permute-start | bytes 786440 | tf_op jit(solution)/shard_map/ppermute | solution.py:25
  23.7 0.1 select_convert_fusion
  23.8 2.3 %collective-permute-done.3.refs_2_ = bf16[256,512]{1,0:T(8,128)(2,1)S(1)} collective-permute-done((bf16[256,512]{1,0:T(8,128)(2,1)S(1)}, bf16[256,512]{1,0:T(8,128)(2,1)S(1)}, u32[]{:S(2)}, u32[]{:S(2)}) %collective-permute-start.3) | collective-permute-done | bytes 262176 | tf_op jit(solution)/shard_map/ppermute | solution.py:25
  26.2 0.0 collective-permute-start.6
  26.2 1.0 %pad_maximum_fusion = bf16[256,640]{1,0:T(8,128)(2,1)S(1)} fusion(bf16[256,128]{1,0:T(8,128)(2,1)S(1)} %select_convert_fusion, bf16[256,512]{1,0:T(8,128)(2,1)} %bitcast.7), kind=kLoop, calls=%fused_computation | loop fusion | flops 655360 | bytes 655360 | tf_op jit(solution)/shard_map/concatenate | solution.py:171
  27.2 4.4 %collective-permute-done.7.refs_5_ = bf16[256,512]{1,0:T(8,128)(2,1)S(1)} collective-permute-done((bf16[256,512]{1,0:T(8,128)(2,1)S(1)}, bf16[256,512]{1,0:T(8,128)(2,1)S(1)}, u32[]{:S(2)}, u32[]{:S(2)}) %collective-permute-start.7) | collective-permute-done | bytes 262176 | tf_op jit(solution)/shard_map/ppermute | solution.py:25
  31.5 0.0 collective-permute-start.1
  31.5 4.1 %collective-permute-done.10.refs_3_ = bf16[256,512]{1,0:T(8,128)(2,1)S(1)} collective-permute-done((bf16[256,512]{1,0:T(8,128)(2,1)S(1)}, bf16[256,512]{1,0:T(8,128)(2,1)S(1)}, u32[]{:S(2)}, u32[]{:S(2)}) %collective-permute-start.10) | collective-permute-done | bytes 262176 | tf_op jit(solution)/shard_map/ppermute | solution.py:25
  35.6 4.1 %collective-permute-start.11 = (bf16[256,512]{1,0:T(8,128)(2,1)S(1)}, bf16[256,512]{1,0:T(8,128)(2,1)S(1)}, u32[]{:S(2)}, u32[]{:S(2)}) collective-permute-start(bf16[256,512]{1,0:T(8,128)(2,1)S(1)} %collective-permute-done.10.refs_3_), channel_id=1, source_target_pairs={{0,31},{1,0},{2,1},{3,2},{4,3},{5,4},{6,5},{7,6},{8,7},{9,8},{10,9... | collective-permute-start | bytes 786440 | tf_op jit(solution)/shard_map/ppermute | solution.py:25
  39.7 0.0 collective-permute-done.6.refs_0_
  39.7 0.0 collective-permute-done.8.refs_0_
  39.7 0.0 collective-permute-start.9
  39.7 0.0 collective-permute-done.1
  39.7 0.0 collective-permute-done.2.q_ref
  39.7 2.2 %tiles_0_1_2.1 = (f32[4,1280,128]{2,1,0:T(8,128)S(1)}, f32[4,1280,128]{2,1,0:T(8,128)S(1)}, f32[4,1280,128]{2,1,0:T(8,128)S(1)}) custom-call(bf16[256,128]{1,0:T(8,128)(2,1)S(1)} %slice.8.starts_ref, bf16[256,2560]{1,0:T(8,128)(2,1)S(1)} %collective-permute-done.2.q_ref, bf16[256,512]{1,0:T(8,128)(2,1)S(1)} %collective-permute-done.8.refs_0_, ...), custom_call_target="tpu_custom_call" | custom-call | flops 2013265920 | bytes 8388608 | tf_op jit(solution)/shard_map/tiles_0_1_2/pallas_call | solution.py:132
  41.9 2.6 %collective-permute-done.11.refs_2_ = bf16[256,512]{1,0:T(8,128)(2,1)S(1)} collective-permute-done((bf16[256,512]{1,0:T(8,128)(2,1)S(1)}, bf16[256,512]{1,0:T(8,128)(2,1)S(1)}, u32[]{:S(2)}, u32[]{:S(2)}) %collective-permute-start.11) | collective-permute-done | bytes 262176 | tf_op jit(solution)/shard_map/ppermute | solution.py:25
  44.5 5.5 %collective-permute-done.9.refs_1_ = bf16[256,512]{1,0:T(8,128)(2,1)S(1)} collective-permute-done((bf16[256,512]{1,0:T(8,128)(2,1)S(1)}, bf16[256,512]{1,0:T(8,128)(2,1)S(1)}, u32[]{:S(2)}, u32[]{:S(2)}) %collective-permute-start.9) | collective-permute-done | bytes 262176 | tf_op jit(solution)/shard_map/ppermute | solution.py:25
  50.0 2.2 %tiles_3_4.1 = bf16[256,2560]{1,0:T(8,128)(2,1)} custom-call(bf16[256,128]{1,0:T(8,128)(2,1)S(1)} %slice.8.starts_ref, bf16[256,2560]{1,0:T(8,128)(2,1)S(1)} %collective-permute-done.2.q_ref, bf16[256,512]{1,0:T(8,128)(2,1)S(1)} %collective-permute-done.6.refs_0_, bf16[256,512]{1,0:T(8,128)(2,1)S(1)} %collective-permute-done.9.refs_1_, ...), custom_call_target="tpu_custom_call" | custom-call | flops 1342177280 | bytes 8388608 | tf_op jit(solution)/shard_map/tiles_3_4/pallas_call | solution.py:132
  (5 shorter events, 0.1 us)
Async XLA Ops:
  0.0 13.7 %collective-permute-start = (bf16[256,512]{1,0:T(8,128)(2,1)}, bf16[256,512]{1,0:T(8,128)(2,1)S(1)}, u32[]{:S(2)}, u32[]{:S(2)}) collective-permute-start(bf16[256,512]{1,0:T(8,128)(2,1)} %bitcast.9), channel_id=1, source_target_pairs={{0,33},{1,34},{2,35},{3,36},{4,37},{5,38},{6,39},{7,40},{8,41},{9,... | collective-permute-start | bytes 786440 | tf_op jit(solution)/shard_map/ppermute | solution.py:25
  1.4 18.8 %collective-permute-start.4 = (bf16[256,512]{1,0:T(8,128)(2,1)}, bf16[256,512]{1,0:T(8,128)(2,1)S(1)}, u32[]{:S(2)}, u32[]{:S(2)}) collective-permute-start(bf16[256,512]{1,0:T(8,128)(2,1)} %bitcast.5), channel_id=1, source_target_pairs={{0,38},{1,39},{2,32},{3,33},{4,42},{5,43},{6,44},{7,45},{8,46},{9,... | collective-permute-start | bytes 786440 | tf_op jit(solution)/shard_map/ppermute | solution.py:25
  8.1 12.1 %collective-permute-start.5 = (bf16[256,512]{1,0:T(8,128)(2,1)}, bf16[256,512]{1,0:T(8,128)(2,1)S(1)}, u32[]{:S(2)}, u32[]{:S(2)}) collective-permute-start(bf16[256,512]{1,0:T(8,128)(2,1)} %bitcast.6), channel_id=1, source_target_pairs={{0,33},{1,34},{2,35},{3,36},{4,37},{5,38},{6,39},{7,40},{8,41},{9,... | collective-permute-start | bytes 786440 | tf_op jit(solution)/shard_map/ppermute | solution.py:25
  8.1 31.7 %collective-permute-start.2 = (bf16[256,2560]{1,0:T(8,128)(2,1)}, bf16[256,2560]{1,0:T(8,128)(2,1)S(1)}, u32[]{:S(2)}, u32[]{:S(2)}) collective-permute-start(bf16[256,2560]{1,0:T(8,128)(2,1)} %bitcast.8), channel_id=1, source_target_pairs={{0,32},{1,33},{2,34},{3,35},{4,36},{5,37},{6,38},{7,39},{8,40},{9,... | collective-permute-start | bytes 3932168 | tf_op jit(solution)/shard_map/ppermute | solution.py:25
  13.7 12.5 %collective-permute-start.3 = (bf16[256,512]{1,0:T(8,128)(2,1)S(1)}, bf16[256,512]{1,0:T(8,128)(2,1)S(1)}, u32[]{:S(2)}, u32[]{:S(2)}) collective-permute-start(bf16[256,512]{1,0:T(8,128)(2,1)S(1)} %collective-permute-done.refs_1_), channel_id=1, source_target_pairs={{0,1},{1,2},{2,3},{3,4},{4,5},{5,6},{6,7},{7,8},{8,9},{9,10},{10,1... | collective-permute-start | bytes 786440 | tf_op jit(solution)/shard_map/ppermute | solution.py:25
  14.6 25.1 %collective-permute-start.8 = (bf16[256,512]{1,0:T(8,128)(2,1)}, bf16[256,512]{1,0:T(8,128)(2,1)S(1)}, u32[]{:S(2)}, u32[]{:S(2)}) collective-permute-start(bf16[256,512]{1,0:T(8,128)(2,1)} %bitcast.10), channel_id=1, source_target_pairs={{0,32},{1,33},{2,34},{3,35},{4,36},{5,37},{6,38},{7,39},{8,40},{9,... | collective-permute-start | bytes 786440 | tf_op jit(solution)/shard_map/ppermute | solution.py:25
  20.1 11.4 %collective-permute-start.7 = (bf16[256,512]{1,0:T(8,128)(2,1)S(1)}, bf16[256,512]{1,0:T(8,128)(2,1)S(1)}, u32[]{:S(2)}, u32[]{:S(2)}) collective-permute-start(bf16[256,512]{1,0:T(8,128)(2,1)S(1)} %collective-permute-done.5.refs_4_), channel_id=1, source_target_pairs={{0,1},{1,2},{2,3},{3,4},{4,5},{5,6},{6,7},{7,8},{8,9},{9,10},{10,1... | collective-permute-start | bytes 786440 | tf_op jit(solution)/shard_map/ppermute | solution.py:25
  20.2 15.4 %collective-permute-start.10 = (bf16[256,512]{1,0:T(8,128)(2,1)S(1)}, bf16[256,512]{1,0:T(8,128)(2,1)S(1)}, u32[]{:S(2)}, u32[]{:S(2)}) collective-permute-start(bf16[256,512]{1,0:T(8,128)(2,1)S(1)} %collective-permute-done.4), channel_id=1, source_target_pairs={{0,6},{1,7},{2,0},{3,1},{4,2},{5,3},{6,4},{7,5},{8,14},{9,15},{10,... | collective-permute-start | bytes 786440 | tf_op jit(solution)/shard_map/ppermute | solution.py:25
  26.2 13.5 %collective-permute-start.6 = (bf16[256,512]{1,0:T(8,128)(2,1)S(1)}, bf16[256,512]{1,0:T(8,128)(2,1)S(1)}, u32[]{:S(2)}, u32[]{:S(2)}) collective-permute-start(bf16[256,512]{1,0:T(8,128)(2,1)S(1)} %collective-permute-done.3.refs_2_), channel_id=1, source_target_pairs={{0,1},{1,2},{2,3},{3,4},{4,5},{5,6},{6,7},{7,8},{8,9},{9,10},{10,1... | collective-permute-start | bytes 786440 | tf_op jit(solution)/shard_map/ppermute | solution.py:25
  31.5 8.1 %collective-permute-start.1 = (bf16[256,640]{1,0:T(8,128)(2,1)S(1)}, bf16[256,640]{1,0:T(8,128)(2,1)S(1)}, u32[]{:S(2)}, u32[]{:S(2)}) collective-permute-start(bf16[256,640]{1,0:T(8,128)(2,1)S(1)} %pad_maximum_fusion), channel_id=1, source_target_pairs={{0,32},{1,33},{2,34},{3,35},{4,36},{5,37},{6,38},{7,39},{8,40},{9,... | collective-permute-start | bytes 983048 | tf_op jit(solution)/shard_map/ppermute | solution.py:25
  35.6 8.9 %collective-permute-start.11 = (bf16[256,512]{1,0:T(8,128)(2,1)S(1)}, bf16[256,512]{1,0:T(8,128)(2,1)S(1)}, u32[]{:S(2)}, u32[]{:S(2)}) collective-permute-start(bf16[256,512]{1,0:T(8,128)(2,1)S(1)} %collective-permute-done.10.refs_3_), channel_id=1, source_target_pairs={{0,31},{1,0},{2,1},{3,2},{4,3},{5,4},{6,5},{7,6},{8,7},{9,8},{10,9... | collective-permute-start | bytes 786440 | tf_op jit(solution)/shard_map/ppermute | solution.py:25
  39.7 10.4 %collective-permute-start.9 = (bf16[256,512]{1,0:T(8,128)(2,1)S(1)}, bf16[256,512]{1,0:T(8,128)(2,1)S(1)}, u32[]{:S(2)}, u32[]{:S(2)}) collective-permute-start(bf16[256,512]{1,0:T(8,128)(2,1)S(1)} %collective-permute-done.6.refs_0_), channel_id=1, source_target_pairs={{0,1},{1,2},{2,3},{3,4},{4,5},{5,6},{6,7},{7,8},{8,9},{9,10},{10,1... | collective-permute-start | bytes 786440 | tf_op jit(solution)/shard_map/ppermute | solution.py:25
